TPU v7x, 256 devices: a whole 4x4x8 slice. The times are simulated.
256 devices in a mesh: expert: 8 (over y, x_lo), dp: 32 (over x_hi, z, core).
Axes of the slice: x: 4 (x_hi: 2, x_lo: 2; x = x_hi * 2 + x_lo), y: 4, z: 8, core: 2. Of those that a mesh axis runs over, the one named last changes fastest.
Arguments:
- tokens: bfloat16 [4096, 3072], P(('expert', 'dp')), may hold values from -6 to 6
- cotangent: bfloat16 [4096, 3072], P(('expert', 'dp')), may hold values from -6 to 6
- experts: int32 [4096, 2], P(('expert', 'dp')), may hold values from 0 to 7, all different within a row; in each aligned block of 16 rows (0 to 15, 16 to 31, ...) at most 8 rows name the same one
- gate_weights: float32 [4096, 2], P(('expert', 'dp')), may hold values from 0.1 to 1
- w_up: bfloat16 [8, 3072, 8192], P('expert', None, 'dp'), may hold values from -0.109375 to 0.109375
- master: float32 [8, 8192, 3072], P(None, 'dp', 'expert'), may hold values from -6 to 6
- moment_one: bfloat16 [8, 8192, 3072], P(None, 'dp', 'expert'), may hold values from -18 to 18
- moment_two: bfloat16 [8, 8192, 3072], P(None, 'dp', 'expert'), may hold values from 10 to 100
Outputs:
- new_master: float32 [8, 8192, 3072], P('expert', 'dp')
Inputs may be any that keep to these rules, and one draw needn't show every extreme that they name: Each token names two different experts; the tokens of one device name any expert at most 8 times, a bound that some block reaches.
All inputs are finite; a program needn't handle non-finite values.
Results may differ from a plain program's by a relative error of at most 0.0003.
Values may be sent and summed in bfloat16 or wider, within the bound.
A program may use at most 128 MiB of HBM per device.

v0:
```python
import jax
import jax.numpy as jnp
from jax import lax
from jax.sharding import PartitionSpec as P

CAP = 8
beta_one = 0.9
beta_two = 0.95
corr_one = 1.0 - (0.9**50) ** 2
corr_two = 1.0 - (0.95**50) ** 2
learn_rate = 0.2
weight_decay = 0.1
epsilon = 1e-08


def adam_update(master, moment_one, moment_two, gradient):
    first = beta_one * moment_one.astype(jnp.float32) + (1.0 - beta_one) * gradient
    second = beta_two * moment_two.astype(jnp.float32) + (1.0 - beta_two) * gradient * gradient
    update = first / corr_one / (jnp.sqrt(second / corr_two) + epsilon)
    return master - learn_rate * (update + weight_decay * master)


def body(tokens, cotangent, experts, gate_weights, w_up, master, moment_one, moment_two):
    count_experts = master.shape[0]
    model_width = tokens.shape[1]
    choices_each = experts.shape[1]
    flat_ids = experts.reshape(-1)
    onehot = (flat_ids[:, None] == jnp.arange(count_experts, dtype=jnp.int32)[None, :]).astype(
        jnp.int32
    )
    position = jnp.sum((jnp.cumsum(onehot, axis=0) - 1) * onehot, axis=1)
    target = flat_ids * CAP + position
    placing = (jnp.arange(count_experts * CAP, dtype=jnp.int32)[:, None] == target[None, :]).astype(
        jnp.bfloat16
    )
    token_copies = jnp.repeat(tokens, choices_each, axis=0)
    scaled = (
        jnp.repeat(cotangent.astype(jnp.float32), choices_each, axis=0)
        * gate_weights.reshape(-1)[:, None]
    ).astype(jnp.bfloat16)
    send_tokens = jnp.dot(placing, token_copies, preferred_element_type=jnp.float32).astype(
        jnp.bfloat16
    )
    send_scaled = jnp.dot(placing, scaled, preferred_element_type=jnp.float32).astype(jnp.bfloat16)
    send_tokens = send_tokens.reshape(count_experts, CAP, model_width)
    send_scaled = send_scaled.reshape(count_experts, CAP, model_width)
    got_tokens, got_scaled = (
        lax.all_to_all(send_tokens, "expert", split_axis=0, concat_axis=0, tiled=True),
        lax.all_to_all(send_scaled, "expert", split_axis=0, concat_axis=0, tiled=True),
    )
    got_tokens = got_tokens.reshape(-1, model_width)
    got_scaled = got_scaled.reshape(-1, model_width)
    local_up = w_up[0]
    piece_tokens = lax.all_gather(got_tokens, "dp", axis=0, tiled=True)
    piece_scaled = lax.all_gather(got_scaled, "dp", axis=0, tiled=True)
    hidden = jax.nn.silu(
        jnp.dot(piece_tokens, local_up, preferred_element_type=jnp.float32)
    ).astype(jnp.bfloat16)
    gradient = lax.dot_general(
        hidden, piece_scaled, (((0,), (0,)), ((), ())), preferred_element_type=jnp.float32
    )
    gradient = gradient[None]
    spread = lax.all_to_all(
        gradient.astype(jnp.bfloat16), "expert", split_axis=2, concat_axis=0, tiled=True
    ).astype(gradient.dtype)
    fresh_master = adam_update(master, moment_one, moment_two, spread)
    return lax.all_to_all(fresh_master, "expert", split_axis=0, concat_axis=2, tiled=True)


def solution(mesh):
    placed = (
        P(("expert", "dp"), None),
        P(("expert", "dp"), None),
        P(("expert", "dp"), None),
        P(("expert", "dp"), None),
        P("expert", None, "dp"),
        P(None, "dp", "expert"),
        P(None, "dp", "expert"),
        P(None, "dp", "expert"),
    )
    return jax.shard_map(
        body, mesh=mesh, in_specs=placed, out_specs=P("expert", "dp", None), check_vma=False
    )
```

profile of v0, /device:TPU:1, one launch (start us, length us, event | category | flops | bytes accessed | tf_op | source)
XLA Modules:
  0.0 399.0 jit_solution(3929386972154533601)
XLA Ops:
  6.5 0.9 copy.17
  7.4 0.1 reshape.36
  7.5 0.1 fusion.21
  7.6 0.1 reduce_window_sum.11
  7.7 0.2 select_reduce_fusion
  7.8 1.0 broadcast_in_dim.5
  8.9 0.3 reshape.40
  9.1 0.8 copy.18
  9.9 0.1 mul.66
  10.0 0.3 fusion.2
  10.3 13.6 %all_to_all.37 = bf16[8,8,3072]{2,1,0:T(8,128)(2,1)} all-to-all(bf16[8,8,3072]{2,1,0:T(8,128)(2,1)S(1)} %fusion.2), channel_id=1, replica_groups=mesh['expert'=8,'dp'=32] {'expert'}, dimensions={0} | all-to-all | bytes 786432 | tf_op jit(solution)/shard_map/all_to_all | solution.py:49
  23.9 0.0 all-gather.5.cloned.1.call-update
  23.9 0.0 all-gather.3.cloned.1.call-start
  24.0 0.1 broadcast_in_dim.4
  24.1 0.1 reshape.37
  24.2 0.2 fusion.1
  24.4 10.1 %all_to_all.38 = bf16[8,8,3072]{2,1,0:T(8,128)(2,1)} all-to-all(bf16[8,8,3072]{2,1,0:T(8,128)(2,1)S(1)} %fusion.1), channel_id=1, replica_groups=mesh['expert'=8,'dp'=32] {'expert'}, dimensions={0} | all-to-all | bytes 786432 | tf_op jit(solution)/shard_map/all_to_all | solution.py:48
  34.6 0.0 all-gather.3.cloned.1.call-update
  34.6 109.2 %all-gather.5.cloned.1.call-done = bf16[2048,3072]{1,0:T(8,128)(2,1)} async-done(((bf16[64,3072]{1,0:T(8,128)(2,1)}), bf16[2048,3072]{1,0:T(8,128)(2,1)}) %all-gather.5.cloned.1.call-update) | async-done | bytes 12582928 | tf_op jit(solution)/shard_map/all_gather | solution.py:55
  143.8 117.0 %all-gather.3.cloned.1.call-done = bf16[2048,3072]{1,0:T(8,128)(2,1)} async-done(((bf16[64,3072]{1,0:T(8,128)(2,1)}), bf16[2048,3072]{1,0:T(8,128)(2,1)}) %all-gather.3.cloned.1.call-update) | async-done | bytes 12582928 | tf_op jit(solution)/shard_map/all_gather | solution.py:54
  260.8 0.0 copy-done
  260.8 21.1 %fusion = bf16[1,256,3072]{2,1,0:T(8,128)(2,1)S(1)} fusion(bf16[2048,3072]{1,0:T(8,128)(2,1)} %all-gather.5.cloned.1.call-done, bf16[2048,3072]{1,0:T(8,128)(2,1)} %all-gather.3.cloned.1.call-done, bf16[1,3072,256]{2,1,0:T(8,128)(2,1)S(1)} %copy-done), kind=kOutput, calls=%fused_computation.2 | convolution fusion | flops 6445858816 | bytes 28311552 | tf_op jit(solution)/shard_map/dot_general | solution.py:59
  281.9 5.2 %copy.19 = bf16[1,256,3072]{1,0,2:T(2,128)(2,1)} copy(bf16[1,256,3072]{2,1,0:T(8,128)(2,1)S(1)} %fusion) | data formatting | bytes 3145728 | tf_op jit(solution)/shard_map/convert_element_type | solution.py:64
  287.1 0.5 broadcast.23
  287.6 16.7 %reduce = bf16[3072,256]{1,0:T(8,128)(2,1)S(1)} reduce(bf16[3072,1,256]{2,1,0:T(2,128)(2,1)} %bitcast.40, bf16[]{:T(256)} %broadcast.23), dimensions={1}, to_apply=%bitcast.35.reduce_sub_computation | reduce | bytes 3145730
  304.3 1.8 reshape.45
  306.1 24.6 %all_to_all.39 = bf16[8,2,49152]{2,1,0:T(2,128)(2,1)S(1)} all-to-all(bf16[8,2,49152]{2,1,0:T(2,128)(2,1)} %reshape.45), channel_id=1, replica_groups=mesh['expert'=8,'dp'=32] {'expert'}, dimensions={0} | all-to-all | bytes 3145728 | tf_op jit(solution)/shard_map/all_to_all | solution.py:63
  330.7 3.9 reshape.46
  334.6 8.8 %copy.20 = f32[1,256,8,384]{3,1,2,0:T(8,128)} copy(bf16[1,256,8,384]{1,0,3,2:T(2,128)(2,1)} %bitcast.41) | data formatting | bytes 4718592 | tf_op jit(solution)/shard_map/convert_element_type | solution.py:65
  343.4 5.8 %multiply_subtract_fusion = f32[8,256,384]{2,1,0:T(8,128)S(1)} fusion(f32[8,256,384]{2,1,0:T(8,128)} %param.13, f32[1,256,8,384]{3,1,2,0:T(8,128)} %copy.20, bf16[8,256,384]{2,1,0:T(8,128)(2,1)S(1)} %copy-done.1, bf16[8,256,384]{2,1,0:T(8,128)(2,1)} %param.14), kind=kLoop, calls=%fused_computation.16 | loop fusion | flops 13369344 | bytes 12582912 | tf_op jit(solution)/shard_map/sub | solution.py:20
  349.2 40.9 %all_to_all.40 = f32[8,256,384]{2,1,0:T(8,128)S(1)} all-to-all(f32[8,256,384]{2,1,0:T(8,128)S(1)} %multiply_subtract_fusion), channel_id=1, replica_groups=mesh['expert'=8,'dp'=32] {'expert'}, dimensions={0} | all-to-all | bytes 6291456 | tf_op jit(solution)/shard_map/all_to_all | solution.py:67
  390.1 2.1 copy.22
  (7 shorter events, 0.0 us)
Async XLA Ops:
  6.5 254.3 %copy-start = (bf16[1,3072,256]{2,1,0:T(8,128)(2,1)S(1)}, bf16[1,3072,256]{2,1,0:T(8,128)(2,1)}, u32[]{:S(2)}) copy-start(bf16[1,3072,256]{2,1,0:T(8,128)(2,1)} %param.12) | copy-start | bytes 4718596
  6.5 17.5 %copy-start.2 = (bf16[16,3072]{1,0:T(8,128)(2,1)S(1)}, bf16[16,3072]{1,0:T(8,128)(2,1)}, u32[]{:S(2)}) copy-start(bf16[16,3072]{1,0:T(8,128)(2,1)} %param.8) | copy-start | bytes 294916
  6.5 137.2 %all-gather.5.cloned.1.call-start = ((), (), s32[]{:S(2)}) async-start(), calls=%async_computation.5 | async-start | bytes 12976128 | tf_op jit(solution)/shard_map/all_gather | solution.py:55
  23.9 236.9 %all-gather.3.cloned.1.call-start = ((), (), s32[]{:S(2)}) async-start(), calls=%async_computation.4 | async-start | bytes 12976128 | tf_op jit(solution)/shard_map/all_gather | solution.py:54
  334.6 8.8 %copy-start.1 = (bf16[8,256,384]{2,1,0:T(8,128)(2,1)S(1)}, bf16[8,256,384]{2,1,0:T(8,128)(2,1)}, u32[]{:S(2)}) copy-start(bf16[8,256,384]{2,1,0:T(8,128)(2,1)} %param.15) | copy-start | bytes 4718596
Sparse Core Ops, SparseCore 0:
  24.1 119.6 all-gather.4
  146.5 114.2 all-gather.2
where the time goes:
time: 400 us; the launch traced here: 399 us
  waiting for transfers between devices  226 us (56%)
  blocking collectives  89.2 us (22%)
  local copies, waits for them, and re-layouts  25.5 us (6%)
  other arithmetic  22.8 us (6%)
  matrix products  21.7 us (5%)
  between operations  13.5 us (3%)
    all_gather x1, waiting for transfers between devices, body(): piece_tokens = lax.all_gather(got_tokens, 'dp', axis=0, tiled=True)  117 us
    all_gather x1, waiting for transfers between devices, body(): piece_scaled = lax.all_gather(got_scaled, 'dp', axis=0, tiled=True)  109 us
    all_to_all x1, blocking collectives, body(): lax.all_to_all(fresh_master, 'expert', split_axis=0, concat_axis=2, tiled...  40.9 us
    all_to_all x1, blocking collectives, body(): lax.all_to_all(gradient.astype(jnp.bfloat16), 'expert', split_axis=2, con...  24.6 us
    dot_general x1, matrix products, body(): lax.dot_general(hidden, piece_scaled, (((0,), (0,)), ((), ())), preferred...  21.1 us
    unnamed x1, other arithmetic  16.7 us
    all_to_all x1, blocking collectives, body(): lax.all_to_all(send_scaled, 'expert', split_axis=0, concat_axis=0, tiled=...  13.6 us
    all_to_all x1, blocking collectives, body(): lax.all_to_all(send_tokens, 'expert', split_axis=0, concat_axis=0, tiled=...  10.1 us
  transfers between devices with their start and end apart: 2, of which 2 were waited for; matrix products, arithmetic and copies ran while one was open for 0% of the time, Pallas kernels for 0%

commit v1 on v0

--- a/solution.py
+++ b/solution.py
@@ -60,8 +60,14 @@
         hidden, piece_scaled, (((0,), (0,)), ((), ())), preferred_element_type=jnp.float32
     )
     gradient = gradient[None]
-    spread = lax.all_to_all(
-        gradient.astype(jnp.bfloat16), "expert", split_axis=2, concat_axis=0, tiled=True
+    spread = jnp.concatenate(
+        jax.lax.all_to_all(
+            jnp.stack(jnp.split(gradient.astype(jnp.bfloat16), jax.lax.axis_size("expert"), 2), 0),
+            "expert",
+            0,
+            0,
+        ),
+        0,
     ).astype(gradient.dtype)
     fresh_master = adam_update(master, moment_one, moment_two, spread)
     return lax.all_to_all(fresh_master, "expert", split_axis=0, concat_axis=2, tiled=True)

time: 400 us -> 364 us (0.910)
  other arithmetic: 22.8 us -> 4.37 us
  local copies, waits for them, and re-layouts: 25.5 us -> 9.94 us
    unnamed x1 -> x0, other arithmetic: 16.7 us -> none
    convert_element_type x2 -> x0, local copies, waits for them, and re-layouts: 14 us -> none  [the longest x1 8.81 us: body(): spread = lax.all_to_all(gradient.astype(jnp.bfloat16), 'expert', split_ax...]
    all_gather x1, waiting for transfers between devices: 117 us -> 109 us  [body(): piece_tokens = lax.all_gather(got_tokens, 'dp', axis=0, tiled=True)]
    all_gather x1, waiting for transfers between devices: 109 us -> 117 us  [body(): piece_scaled = lax.all_gather(got_scaled, 'dp', axis=0, tiled=True)]
    unnamed x11 -> x19, local copies, waits for them, and re-layouts: 7.86 us -> 1.19 us
    all_to_all x1 -> x2, local copies, waits for them, and re-layouts: 2.06 us -> 7.09 us  [body(): lax.all_to_all(fresh_master, 'expert', split_axis=0, concat_axis=2, tiled...]
where the time goes in v1:
time: 364 us
  waiting for transfers between devices  226 us (62%)
  blocking collectives  88.3 us (24%)
  matrix products  21.7 us (6%)
  between operations  13.6 us (4%)
  local copies, waits for them, and re-layouts  9.94 us (3%)
  other arithmetic  4.37 us (1%)
    all_gather x1, waiting for transfers between devices, body(): piece_scaled = lax.all_gather(got_scaled, 'dp', axis=0, tiled=True)  117 us
    all_gather x1, waiting for transfers between devices, body(): piece_tokens = lax.all_gather(got_tokens, 'dp', axis=0, tiled=True)  109 us
    all_to_all x1, blocking collectives, body(): lax.all_to_all(fresh_master, 'expert', split_axis=0, concat_axis=2, tiled...  39.9 us
    all_to_all x1, blocking collectives, body(): jax.lax.all_to_all(jnp.stack(jnp.split(gradient.astype(jnp.bfloat16), jax...  24.7 us
    dot_general x1, matrix products, body(): lax.dot_general(hidden, piece_scaled, (((0,), (0,)), ((), ())), preferred...  21.1 us
    all_to_all x1, blocking collectives, body(): lax.all_to_all(send_tokens, 'expert', split_axis=0, concat_axis=0, tiled=...  13.6 us
    all_to_all x1, blocking collectives, body(): lax.all_to_all(send_scaled, 'expert', split_axis=0, concat_axis=0, tiled=...  10.1 us
  transfers between devices with their start and end apart: 2, of which 2 were waited for; matrix products, arithmetic and copies ran while one was open for 0% of the time, Pallas kernels for 0%

profile of v1, /device:TPU:1, one launch (start us, length us, event | category | flops | bytes accessed | tf_op | source)
XLA Modules:
  0.0 363.7 jit_solution(12717505095565510971)
XLA Ops:
  6.5 0.0 copy-start
  6.5 0.0 all-gather.3.cloned.1.call-start
  6.5 0.9 copy.11
  7.4 0.1 reshape.35
  7.5 0.1 fusion.31
  7.6 0.1 reduce_window_sum.11
  7.6 0.2 select_reduce_fusion
  7.8 1.0 broadcast_in_dim.4
  8.8 0.1 reshape.36
  8.9 0.2 fusion.1
  9.2 13.6 %all_to_all.33 = bf16[8,8,3072]{2,1,0:T(8,128)(2,1)} all-to-all(bf16[8,8,3072]{2,1,0:T(8,128)(2,1)S(1)} %fusion.1), channel_id=1, replica_groups=mesh['expert'=8,'dp'=32] {'expert'}, dimensions={0} | all-to-all | bytes 786432 | tf_op jit(solution)/shard_map/all_to_all | solution.py:48
  22.8 0.0 all-gather.3.cloned.1.call-update
  22.8 0.0 all-gather.5.cloned.1.call-start
  22.8 0.0 copy-done.4
  22.9 0.1 copy.12
  22.9 0.1 mul.66
  23.0 0.0 copy-done.3
  23.0 0.1 broadcast_in_dim.5
  23.2 0.3 reshape.39
  23.4 0.3 fusion.2
  23.8 10.1 %all_to_all.34 = bf16[8,8,3072]{2,1,0:T(8,128)(2,1)} all-to-all(bf16[8,8,3072]{2,1,0:T(8,128)(2,1)S(1)} %fusion.2), channel_id=1, replica_groups=mesh['expert'=8,'dp'=32] {'expert'}, dimensions={0} | all-to-all | bytes 786432 | tf_op jit(solution)/shard_map/all_to_all | solution.py:49
  33.9 0.0 all-gather.5.cloned.1.call-update
  33.9 108.7 %all-gather.3.cloned.1.call-done = bf16[2048,3072]{1,0:T(8,128)(2,1)} async-done(((bf16[64,3072]{1,0:T(8,128)(2,1)}), bf16[2048,3072]{1,0:T(8,128)(2,1)}) %all-gather.3.cloned.1.call-update) | async-done | bytes 12582928 | tf_op jit(solution)/shard_map/all_gather | solution.py:54
  142.6 117.0 %all-gather.5.cloned.1.call-done = bf16[2048,3072]{1,0:T(8,128)(2,1)} async-done(((bf16[64,3072]{1,0:T(8,128)(2,1)}), bf16[2048,3072]{1,0:T(8,128)(2,1)}) %all-gather.5.cloned.1.call-update) | async-done | bytes 12582928 | tf_op jit(solution)/shard_map/all_gather | solution.py:55
  259.7 21.1 %fusion = bf16[1,256,3072]{2,1,0:T(8,128)(2,1)S(1)} fusion(bf16[2048,3072]{1,0:T(8,128)(2,1)} %all-gather.5.cloned.1.call-done, bf16[2048,3072]{1,0:T(8,128)(2,1)} %all-gather.3.cloned.1.call-done, bf16[1,3072,256]{2,1,0:T(8,128)(2,1)S(1)} %copy-done), kind=kOutput, calls=%fused_computation.4 | convolution fusion | flops 6445858816 | bytes 28311552 | tf_op jit(solution)/shard_map/dot_general | solution.py:59
  280.9 0.0 copy-start.2
  281.0 0.0 copy-start.1
  281.1 24.7 %all_to_all.35 = bf16[8,1,256,384]{3,2,1,0:T(8,128)(2,1)S(1)} all-to-all(bf16[8,1,256,384]{3,2,1,0:T(8,128)(2,1)S(1)} %fusion.20), channel_id=1, replica_groups=mesh['expert'=8,'dp'=32] {'expert'}, dimensions={0} | all-to-all | bytes 3145728 | tf_op jit(solution)/shard_map/all_to_all | solution.py:64
  305.8 4.1 %fusion.8 = f32[8,256,384]{2,1,0:T(8,128)S(1)} fusion(f32[8,256,384]{2,1,0:T(8,128)S(1)} %copy-done.1, bf16[8,256,384]{2,1,0:T(8,128)(2,1)S(1)} %copy-done.2, bf16[8,256,384]{2,1,0:T(8,128)(2,1)} %param.14, bf16[8,1,256,384]{3,2,1,0:T(8,128)(2,1)S(1)} %all_to_all.35), kind=kLoop, calls=%fused_computation.14 | loop fusion | flops 14155776 | bytes 11010048 | tf_op jit(solution)/shard_map/sub | solution.py:20
  309.8 39.9 %all_to_all.36 = f32[8,256,384]{2,1,0:T(8,128)} all-to-all(f32[8,256,384]{2,1,0:T(8,128)S(1)} %fusion.8), channel_id=1, replica_groups=mesh['expert'=8,'dp'=32] {'expert'}, dimensions={0} | all-to-all | bytes 6291456 | tf_op jit(solution)/shard_map/all_to_all | solution.py:73
  349.7 3.6 copy.13
  353.3 3.5 copy.14
  (14 shorter events, 0.3 us)
Async XLA Ops:
  6.5 253.1 %copy-start = (bf16[1,3072,256]{2,1,0:T(8,128)(2,1)S(1)}, bf16[1,3072,256]{2,1,0:T(8,128)(2,1)}, u32[]{:S(2)}) copy-start(bf16[1,3072,256]{2,1,0:T(8,128)(2,1)} %param.12) | copy-start | bytes 4718596
  6.5 16.3 %copy-start.4 = (f32[16,2]{0,1:T(2,128)S(1)}, f32[16,2]{0,1:T(2,128)}, u32[]{:S(2)}) copy-start(f32[16,2]{0,1:T(2,128)} %param.11) | copy-start | bytes 388
  6.5 16.5 %copy-start.3 = (bf16[16,3072]{1,0:T(8,128)(2,1)S(1)}, bf16[16,3072]{1,0:T(8,128)(2,1)}, u32[]{:S(2)}) copy-start(bf16[16,3072]{1,0:T(8,128)(2,1)} %param.9) | copy-start | bytes 294916
  6.5 136.1 %all-gather.3.cloned.1.call-start = ((), (), s32[]{:S(2)}) async-start(), calls=%async_computation.4 | async-start | bytes 12976128 | tf_op jit(solution)/shard_map/all_gather | solution.py:54
  22.8 236.9 %all-gather.5.cloned.1.call-start = ((), (), s32[]{:S(2)}) async-start(), calls=%async_computation.5 | async-start | bytes 12976128 | tf_op jit(solution)/shard_map/all_gather | solution.py:55
  280.9 24.9 %copy-start.2 = (bf16[8,256,384]{2,1,0:T(8,128)(2,1)S(1)}, bf16[8,256,384]{2,1,0:T(8,128)(2,1)}, u32[]{:S(2)}) copy-start(bf16[8,256,384]{2,1,0:T(8,128)(2,1)} %param.15) | copy-start | bytes 4718596
  281.0 24.8 %copy-start.1 = (f32[8,256,384]{2,1,0:T(8,128)S(1)}, f32[8,256,384]{2,1,0:T(8,128)}, u32[]{:S(2)}) copy-start(f32[8,256,384]{2,1,0:T(8,128)} %param.13) | copy-start | bytes 9437188
Sparse Core Ops, SparseCore 0:
  22.9 119.6 all-gather.2
  145.4 114.2 all-gather.4
